TPU v7x, 128 devices: a whole 4x4x4 slice. The times are simulated.
128 devices in a mesh: branch: 2 (over x_lo), row: 4 (over z), col: 16 (over x_hi, y, core).
Axes of the slice: x: 4 (x_hi: 2, x_lo: 2; x = x_hi * 2 + x_lo), y: 4, z: 4, core: 2. Of those that a mesh axis runs over, the one named last changes fastest.
Arguments:
- x_act: bfloat16 [2, 1024, 5120], P('branch', 'row', 'col'), may hold values from -6 to 6
- grad_out: bfloat16 [2, 1024, 5120], P('branch', 'row', 'col'), may hold values from -6 to 6
- w_gate: bfloat16 [5120, 8192], P('row', 'col'), may hold values from -0.078125 to 0.078125
- w_up: bfloat16 [5120, 8192], P('row', 'col'), may hold values from -0.078125 to 0.078125
- w_down: bfloat16 [8192, 5120], P('col', 'row'), may hold values from -0.0625 to 0.0625
Outputs:
- out_act: bfloat16 [2, 1024, 5120], P('branch', 'row', 'col')
- grad_in: bfloat16 [2, 1024, 5120], P('branch', 'row', 'col')
- grad_gate: float32 [5120, 8192], P('row', 'col')
- grad_up: float32 [5120, 8192], P('row', 'col')
- grad_down: float32 [8192, 5120], P('col', 'row')
All inputs are finite; a program needn't handle non-finite values.
Results may differ from a plain program's by a relative error of at most 0.019.
Values may be sent and summed in bfloat16 or wider, within the bound.
A program may use at most 128 MiB of HBM per device.

v0:
```python
import jax
import jax.numpy as jnp
from jax import lax
from jax.sharding import PartitionSpec as P


def contract_rows(left, right):
    return lax.dot_general(
        left, right, (((0,), (0,)), ((), ())), preferred_element_type=jnp.float32
    )


def contract_cols(left, right):
    return lax.dot_general(
        left, right, (((1,), (1,)), ((), ())), preferred_element_type=jnp.float32
    )


def body(x_act, grad_out, w_gate, w_up, w_down):
    tok_rows, dy_rows = (
        lax.all_gather(x_act[0], "col", axis=1, tiled=True),
        lax.all_gather(grad_out[0], "col", axis=1, tiled=True),
    )
    stacked = jnp.stack([w_gate, w_up])
    panels = lax.all_gather(stacked, "row", axis=1, tiled=True)
    gate = jnp.dot(tok_rows, panels[0], preferred_element_type=jnp.float32)
    up = jnp.dot(tok_rows, panels[1], preferred_element_type=jnp.float32)
    down_full = lax.all_gather(w_down, "row", axis=1, tiled=True)
    sig = jax.nn.sigmoid(gate)
    swish = gate * sig
    hidden = (swish * up).astype(jnp.bfloat16)
    out_terms = jnp.dot(hidden, down_full, preferred_element_type=jnp.float32)
    out_rows = lax.psum_scatter(
        out_terms.astype(jnp.bfloat16), "col", scatter_dimension=1, tiled=True
    )
    d_hidden = contract_cols(dy_rows, down_full)
    d_gate = (d_hidden * up * sig * (1.0 + gate * (1.0 - sig))).astype(jnp.bfloat16)
    d_up = (d_hidden * swish).astype(jnp.bfloat16)
    dx_terms = contract_cols(d_gate, panels[0]) + contract_cols(d_up, panels[1])
    dx_rows = lax.psum_scatter(
        dx_terms.astype(jnp.bfloat16), "col", scatter_dimension=1, tiled=True
    )
    n_rows = lax.axis_size("row")
    n_passes = lax.axis_size("branch")

    def order_lead(term):
        lead = term.shape[0]
        shaped = term.reshape(n_rows, n_passes, lead // (n_rows * n_passes), term.shape[1])
        return shaped.transpose(1, 0, 2, 3).reshape(lead, term.shape[1])

    gate_term = order_lead(contract_rows(tok_rows, d_gate))
    up_term = order_lead(contract_rows(tok_rows, d_up))
    term = contract_rows(hidden, dy_rows)
    tail = term.shape[1]
    shaped = term.reshape(term.shape[0], n_rows, n_passes, tail // (n_rows * n_passes))
    down_term = shaped.transpose(0, 2, 1, 3).reshape(term.shape[0], tail)
    part_gate, part_up = (
        lax.psum_scatter(
            gate_term.astype(jnp.bfloat16), ("branch", "row"), scatter_dimension=0, tiled=True
        ).astype(jnp.float32),
        lax.psum_scatter(
            up_term.astype(jnp.bfloat16), ("branch", "row"), scatter_dimension=0, tiled=True
        ).astype(jnp.float32),
    )
    part_down = lax.psum_scatter(
        down_term.astype(jnp.bfloat16), ("branch", "row"), scatter_dimension=1, tiled=True
    ).astype(jnp.float32)
    grad_gate, grad_up, grad_down = (
        lax.all_gather(part_gate.astype(jnp.bfloat16), "branch", axis=0, tiled=True).astype(
            part_gate.dtype
        ),
        lax.all_gather(part_up.astype(jnp.bfloat16), "branch", axis=0, tiled=True).astype(
            part_up.dtype
        ),
        lax.all_gather(part_down.astype(jnp.bfloat16), "branch", axis=1, tiled=True).astype(
            part_down.dtype
        ),
    )
    return (out_rows[None], dx_rows[None], grad_gate, grad_up, grad_down)


def solution(mesh):
    placed = (
        P("branch", "row", "col"),
        P("branch", "row", "col"),
        P("row", "col"),
        P("row", "col"),
        P("col", "row"),
    )
    return jax.shard_map(
        body,
        mesh=mesh,
        in_specs=placed,
        out_specs=(
            P("branch", "row", "col"),
            P("branch", "row", "col"),
            P("row", "col"),
            P("row", "col"),
            P("col", "row"),
        ),
        check_vma=False,
    )
```

profile of v0, /device:TPU:66, one launch (start us, length us, event | category | flops | bytes accessed | tf_op | source)
XLA Modules:
  0.0 748.3 jit_solution(1893388671434068180)
XLA Ops:
  7.9 3.4 pad_maximum_fusion
  12.8 47.5 %all-gather.20.cloned.1.call-done = bf16[1,256,5120]{1,2,0:T(8,128)(2,1)} async-done(((bf16[1,256,320]{1,2,0:T(8,128)(2,1)}), bf16[1,256,5120]{1,2,0:T(8,128)(2,1)}) %all-gather.20.cloned.1.call-update) | async-done | bytes 2621456 | tf_op jit(solution)/shard_map/all_gather | solution.py:21
  60.3 102.6 %all-gather.10.cloned.1.call-done = bf16[2,5120,512]{2,1,0:T(8,128)(2,1)} async-done(((bf16[2,1280,512]{2,1,0:T(8,128)(2,1)}), bf16[2,5120,512]{2,1,0:T(8,128)(2,1)}) %all-gather.10.cloned.1.call-update) | async-done | bytes 10485776 | tf_op jit(solution)/shard_map/all_gather | solution.py:25
  162.9 5.8 fusion.16
  169.4 2.3 fusion.13
  171.7 43.1 %all-gather.22.cloned.1.call-done = bf16[1,256,5120]{1,2,0:T(8,128)(2,1)} async-done(((bf16[1,256,320]{1,2,0:T(8,128)(2,1)}), bf16[1,256,5120]{1,2,0:T(8,128)(2,1)}) %all-gather.22.cloned.1.call-update) | async-done | bytes 2621456 | tf_op jit(solution)/shard_map/all_gather | solution.py:22
  214.8 57.6 %all-gather.12.cloned.1.call-done = bf16[512,5120]{1,0:T(8,128)(2,1)} async-done(((bf16[512,1280]{1,0:T(8,128)(2,1)}), bf16[512,5120]{1,0:T(8,128)(2,1)}) %all-gather.12.cloned.1.call-update) | async-done | bytes 5242896 | tf_op jit(solution)/shard_map/all_gather | solution.py:28
  272.4 5.1 multiply_convert_fusion
  277.5 3.8 fusion
  281.3 12.5 %convert_element_type.79 = bf16[4,2,640,512]{2,1,0,3:T(2,128)(2,1)} reshape(bf16[5120,512]{0,1:T(8,128)(2,1)} %fusion) | data formatting | bytes 10485760 | tf_op jit(solution)/shard_map/convert_element_type | solution.py:59
  293.8 13.6 %copy.17 = bf16[2,4,640,512]{3,2,1,0:T(8,128)(2,1)} copy(bf16[2,4,640,512]{2,0,1,3:T(2,128)(2,1)} %bitcast.68) | data formatting | bytes 10485760 | tf_op jit(solution)/shard_map/convert_element_type | solution.py:59
  307.4 3.9 fusion.1
  311.4 12.5 %convert_element_type.85 = bf16[4,2,640,512]{2,1,0,3:T(2,128)(2,1)} reshape(bf16[5120,512]{0,1:T(8,128)(2,1)} %fusion.1) | data formatting | bytes 10485760 | tf_op jit(solution)/shard_map/convert_element_type | solution.py:62
  323.8 13.7 %copy.18 = bf16[2,4,640,512]{3,2,1,0:T(8,128)(2,1)} copy(bf16[2,4,640,512]{2,0,1,3:T(2,128)(2,1)} %bitcast.69) | data formatting | bytes 10485760 | tf_op jit(solution)/shard_map/convert_element_type | solution.py:62
  337.8 1.5 copy-done.2
  339.3 4.0 convolution_convert_fusion
  343.3 12.5 %convert_element_type.90 = bf16[512,4,2,640]{3,2,1,0:T(2,128)(2,1)} reshape(bf16[512,5120]{1,0:T(8,128)(2,1)} %convolution_convert_fusion) | data formatting | bytes 10485760 | tf_op jit(solution)/shard_map/convert_element_type | solution.py:66
  355.7 13.6 %copy.23 = bf16[512,2,4,640]{0,3,2,1:T(8,128)(2,1)} copy(bf16[512,2,4,640]{3,1,2,0:T(2,128)(2,1)} %bitcast.70) | data formatting | bytes 10485760
  370.2 63.4 %reduce-scatter.14.cloned.1.call-done = bf16[640,512]{1,0:T(8,128)(2,1)} async-done(((bf16[5120,512]{1,0:T(8,128)(2,1)}), bf16[640,512]{1,0:T(8,128)(2,1)}) %reduce-scatter.14.cloned.1.call-update) | async-done | bytes 655376 | tf_op jit(solution)/shard_map/reduce_scatter | solution.py:61
  433.6 64.2 %reduce-scatter.16.cloned.1.call-done = bf16[640,512]{1,0:T(8,128)(2,1)} async-done(((bf16[5120,512]{1,0:T(8,128)(2,1)}), bf16[640,512]{1,0:T(8,128)(2,1)}) %reduce-scatter.16.cloned.1.call-update) | async-done | bytes 655376
  497.9 2.2 copy.22
  500.1 6.1 convolution_convert_fusion.3
  506.3 4.0 fusion.3
  510.3 5.9 fusion.2
  516.2 10.4 %all-gather.14.cloned.1.call-done = bf16[1280,512]{1,0:T(8,128)(2,1)} async-done(((bf16[640,512]{1,0:T(8,128)(2,1)}), bf16[1280,512]{1,0:T(8,128)(2,1)}) %all-gather.14.cloned.1.call-update) | async-done | bytes 1310736 | tf_op jit(solution)/shard_map/all_gather | solution.py:69
  526.7 3.2 convert_element_type.82
  529.8 26.3 %all-gather.16.cloned.1.call-done = bf16[1280,512]{1,0:T(8,128)(2,1)} async-done(((bf16[640,512]{1,0:T(8,128)(2,1)}), bf16[1280,512]{1,0:T(8,128)(2,1)}) %all-gather.16.cloned.1.call-update) | async-done | bytes 1310736 | tf_op jit(solution)/shard_map/all_gather | solution.py:72
  556.1 3.2 convert_element_type.88
  559.3 26.7 %all-gather.18.cloned.1.call-done = bf16[512,1280]{1,0:T(8,128)(2,1)} async-done(((bf16[512,640]{1,0:T(8,128)(2,1)}), bf16[512,1280]{1,0:T(8,128)(2,1)}) %all-gather.18.cloned.1.call-update) | async-done | bytes 1310736 | tf_op jit(solution)/shard_map/all_gather | solution.py:75
  585.9 3.0 convert_element_type.93
  588.9 75.8 %reduce-scatter.8.cloned.1.call-done = bf16[256,320]{0,1:T(8,128)(2,1)} async-done(((bf16[256,5120]{0,1:T(8,128)(2,1)}), bf16[256,320]{0,1:T(8,128)(2,1)}) %reduce-scatter.8.cloned.1.call-update) | async-done | bytes 163856 | tf_op jit(solution)/shard_map/reduce_scatter | solution.py:33
  664.8 76.7 %reduce-scatter.10.cloned.1.call-done = bf16[256,320]{0,1:T(8,128)(2,1)} async-done(((bf16[256,5120]{0,1:T(8,128)(2,1)}), bf16[256,320]{0,1:T(8,128)(2,1)}) %reduce-scatter.10.cloned.1.call-update) | async-done | bytes 163856 | tf_op jit(solution)/shard_map/reduce_scatter | solution.py:40
  (30 shorter events, 4.0 us)
Async XLA Ops:
  7.2 53.1 %all-gather.20.cloned.1.call-start = ((), (), s32[]{:S(2)}) async-start(), calls=%async_computation.14 | async-start | bytes 2785280 | tf_op jit(solution)/shard_map/all_gather | solution.py:21
  7.9 155.0 %all-gather.10.cloned.1.call-start = ((), (), s32[]{:S(2)}) async-start(), calls=%async_computation.5 | async-start | bytes 13107200 | tf_op jit(solution)/shard_map/all_gather | solution.py:25
  11.4 203.4 %all-gather.22.cloned.1.call-start = ((), (), s32[]{:S(2)}) async-start(), calls=%async_computation.15 | async-start | bytes 2785280 | tf_op jit(solution)/shard_map/all_gather | solution.py:22
  12.2 260.2 %all-gather.12.cloned.1.call-start = ((), (), s32[]{:S(2)}) async-start(), calls=%async_computation.6 | async-start | bytes 6553600 | tf_op jit(solution)/shard_map/all_gather | solution.py:28
  12.7 356.7 %reduce-scatter.12.cloned.1.call-start = ((), (), s32[]{:S(2)}) async-start(), calls=%async_computation.9 | async-start | bytes 5898240 | tf_op jit(solution)/shard_map/reduce_scatter | solution.py:58
  60.3 108.4 %copy-start.1 = (bf16[1,256,5120]{1,2,0:T(8,128)(2,1)S(1)}, bf16[1,256,5120]{1,2,0:T(8,128)(2,1)}, u32[]{:S(2)}) copy-start(bf16[1,256,5120]{1,2,0:T(8,128)(2,1)} %all-gather.20.cloned.1.call-done) | copy-start | bytes 7864324
  162.9 6.5 copy-start
  307.4 126.2 %reduce-scatter.14.cloned.1.call-start = ((), (), s32[]{:S(2)}) async-start(), calls=%async_computation.11 | async-start | bytes 5898240 | tf_op jit(solution)/shard_map/reduce_scatter | solution.py:61
  337.5 1.8 copy-start.2
  337.6 160.3 %reduce-scatter.16.cloned.1.call-start = ((), (), s32[]{:S(2)}) async-start(), calls=%async_computation.16 | async-start | bytes 5898240
  369.4 157.3 %all-gather.14.cloned.1.call-start = ((), (), s32[]{:S(2)}) async-start(), calls=%async_computation.10 | async-start | bytes 1966080 | tf_op jit(solution)/shard_map/all_gather | solution.py:69
  370.2 185.9 %all-gather.16.cloned.1.call-start = ((), (), s32[]{:S(2)}) async-start(), calls=%async_computation.12 | async-start | bytes 1966080 | tf_op jit(solution)/shard_map/all_gather | solution.py:72
  433.6 152.4 %all-gather.18.cloned.1.call-start = ((), (), s32[]{:S(2)}) async-start(), calls=%async_computation.13 | async-start | bytes 1966080 | tf_op jit(solution)/shard_map/all_gather | solution.py:75
  500.0 164.7 %reduce-scatter.8.cloned.1.call-start = ((), (), s32[]{:S(2)}) async-start(), calls=%async_computation.7 | async-start | bytes 2785280 | tf_op jit(solution)/shard_map/reduce_scatter | solution.py:33
  506.2 235.2 %reduce-scatter.10.cloned.1.call-start = ((), (), s32[]{:S(2)}) async-start(), calls=%async_computation.8 | async-start | bytes 2785280 | tf_op jit(solution)/shard_map/reduce_scatter | solution.py:40
Sparse Core Ops, SparseCore 0:
  10.5 49.7 all-gather.19
  62.5 100.3 all-gather.9
  165.4 49.3 all-gather.21
  216.3 55.9 all-gather.11
  307.5 61.8 reduce-scatter.11
  371.7 61.8 reduce-scatter.13
  436.0 61.8 reduce-scatter.15
  499.5 27.1 all-gather.13
  528.3 27.7 all-gather.15
  558.2 27.7 all-gather.17
  590.5 74.2 reduce-scatter.7
  669.2 72.1 reduce-scatter.9
where the time goes:
time: 752 us; the launch traced here: 748 us
  waiting for transfers between devices  597 us (79%)
  local copies, waits for them, and re-layouts  82.7 us (11%)
  matrix products  41 us (5%)
  between operations  14.2 us (2%)
  other arithmetic  12.8 us (2%)
    all_gather x1, waiting for transfers between devices, body(): panels = lax.all_gather(stacked, 'row', axis=1, tiled=True)  103 us
    reduce_scatter x1, waiting for transfers between devices, body(): lax.psum_scatter(dx_terms.astype(jnp.bfloat16), 'col', scatter_dimension=...  76.7 us
    reduce_scatter x1, waiting for transfers between devices, body(): lax.psum_scatter(out_terms.astype(jnp.bfloat16), 'col', scatter_dimension...  75.8 us
    unnamed x13, waiting for transfers between devices  66.9 us
    reduce_scatter x1, waiting for transfers between devices, body(): lax.psum_scatter(up_term.astype(jnp.bfloat16), ('branch', 'row'), scatter...  63.4 us
    all_gather x1, waiting for transfers between devices, body(): down_full = lax.all_gather(w_down, 'row', axis=1, tiled=True)  57.6 us
    all_gather x1, waiting for transfers between devices, body(): lax.all_gather(x_act[0], 'col', axis=1, tiled=True)  47.5 us
    all_gather x1, waiting for transfers between devices, body(): lax.all_gather(grad_out[0], 'col', axis=1, tiled=True)  43.1 us
  transfers between devices with their start and end apart: 12, of which 11 were waited for; matrix products, arithmetic and copies ran while one was open for 13% of the time, Pallas kernels for 0%

commit v1 on v0

v1 whole, which is shorter than its diff:
```python
import functools

import jax
import jax.numpy as jnp
from jax import lax
from jax.experimental import pallas as pl
from jax.experimental.pallas import tpu as pltpu
from jax.sharding import PartitionSpec as P

MESH = pl.DeviceIdType.MESH
BF16 = jnp.bfloat16
F32 = jnp.float32

N_ROW = 4
FEAT = 320
TOK = 256
PANEL = 1280
HID = 512
NQ = 4
HC = HID // NQ


def dot_nn(left, right):
    return jnp.dot(left, right, preferred_element_type=F32)


def dot_nt(left, right):
    return lax.dot_general(left, right, (((1,), (1,)), ((), ())), preferred_element_type=F32)


def layer_kernel(
    x_in, dy_in, wg, wu, wd,
    out_t, dx_t, own_gu, got_gu, own_dn, got_dn,
    xs, wgut, wdt,
    p_gu, r_gu, o_gu, p_dh, r_dh, o_dh, c_gate, c_up,
    hid, dgu, g_gu, g_dn,
    o_part, o_sib, o_sum, o_y, o_fin, o_got,
    p0_s, p0_r, p1_s, p1_r, p2_s, p2_r,
    gu_s, gu_r, hb_s, hb_r, dh_s, dh_r, dg_s, dg_r,
    xd_s, xd_r, xg_s, xg_r, loc_d, loc_g,
    sb_s, sb_r, yr_s, yr_r, fn_s, fn_r,
):
    b, z, c = lax.axis_index("branch"), lax.axis_index("row"), lax.axis_index("col")
    y, xh, sub, core = (c // 2) % 4, c // 8, c % 4, c % 2
    yh = y // 2
    home = c // 4 == z

    def at_z(d):
        return (b, (z + d) % N_ROW, c)

    def at_y(d):
        return (b, z, xh * 8 + ((y + d) % 4) * 2 + core)

    sibling = (b, z, c + 1 - 2 * core)
    partner = (1 - b, z, c)

    def spread_to(h):
        return (b, c // 4, h * 8 + (z % 2) * 4 + sub)

    def spread_from(i):
        return (b, 2 * i + yh, 4 * z + sub)

    def rows_of(j):
        return pl.ds(pl.multiple_of(j * FEAT, 64), FEAT)

    def remote(src, dst, ssem, rsem, to):
        return pltpu.make_async_remote_copy(
            src_ref=src, dst_ref=dst, send_sem=ssem, recv_sem=rsem, device_id=to, device_id_type=MESH
        )

    barrier = pltpu.get_barrier_semaphore()
    for to in [at_z(1), at_z(2), at_z(3), at_y(1), at_y(2), at_y(3), sibling, partner]:
        pl.semaphore_signal(barrier, inc=1, device_id=to, device_id_type=MESH)
    for i in range(2):
        @pl.when(jnp.logical_not(home & (xh == i)))
        def _(i=i):
            pl.semaphore_signal(barrier, inc=1, device_id=spread_to(i), device_id_type=MESH)
            pl.semaphore_signal(barrier, inc=1, device_id=spread_from(i), device_id_type=MESH)

    pl.semaphore_wait(barrier, jnp.where(home, 10, 12))

    acts = (x_in, dy_in)

    def spread_copy(s, h):
        return remote(
            acts[s], xs.at[s, z // 2, z % 2, rows_of(sub)], p0_s.at[s, h], p0_r.at[s, z // 2], spread_to(h)
        )

    def spread_local(s):
        return pltpu.make_async_copy(
            acts[s], xs.at[s, z // 2, z % 2, rows_of(sub)], p0_r.at[s, z // 2]
        )

    def spread_start(s):
        for h in range(2):
            @pl.when(jnp.logical_not(home & (xh == h)))
            def _(h=h):
                spread_copy(s, h).start()

        @pl.when(home)
        def _():
            spread_local(s).start()

    def spread_wait_recv(s):
        for i in range(2):
            pltpu.make_async_copy(
                acts[s], xs.at[s, i, yh, rows_of(sub)], p0_r.at[s, i]
            ).wait()

    def spread_wait_send(s):
        for h in range(2):
            @pl.when(jnp.logical_not(home & (xh == h)))
            def _(h=h):
                spread_copy(s, h).wait_send()

    def group(s, d):
        yy = (y - d + 4) % 4
        return xs.at[s, :, yy // 2, rows_of(2 * (yy % 2) + core)]

    def y_copy(s, d):
        return remote(group(s, 0), group(s, 0), p1_s.at[s, d - 1], p1_r.at[s, d - 1], at_y(d))

    def y_wait_recv(s, d):
        remote(group(s, 0), group(s, d), p1_s.at[s, d - 1], p1_r.at[s, d - 1], at_y(d)).wait_recv()

    def sib_copy(s, d):
        return remote(group(s, d), group(s, d), p2_s.at[s, d], p2_r.at[s, d], sibling)

    def sib_wait_recv(s):
        for d in range(4):
            yy = (y - d + 4) % 4
            there = xs.at[s, :, yy // 2, rows_of(2 * (yy % 2) + 1 - core)]
            remote(group(s, d), there, p2_s.at[s, d], p2_r.at[s, d], sibling).wait_recv()

    def gather_start(s):
        for d in (2, 1, 3):
            y_copy(s, d).start()
        sib_copy(s, 0).start()

    def gather_forward(s):
        for d in (1, 3, 2):
            y_wait_recv(s, d)
            sib_copy(s, d).start()

    spread_start(0)
    spread_start(1)

    @pl.loop(0, NQ)
    def _(q):
        cols = pl.ds(pl.multiple_of(q * HC, HC), HC)
        wgut[pl.ds(pl.multiple_of(q * 2 * HC, HC), HC), :] = wg[:, cols].T
        wgut[pl.ds(pl.multiple_of(q * 2 * HC + HC, HC), HC), :] = wu[:, cols].T

    spread_wait_recv(0)
    gather_start(0)

    @pl.loop(0, NQ)
    def _(q):
        cols = pl.ds(pl.multiple_of(q * HC, HC), HC)
        wdt[:, cols] = wd[cols, :].T

    spread_wait_recv(1)
    for d in (2, 1, 3):
        y_copy(0, d).wait_send()
    gather_start(1)
    gather_forward(0)
    sib_wait_recv(0)

    def z_loop(q, lhs, s, parts, own, send, recv, remote_dst):
        @pl.loop(0, 3)
        def _(i):
            t = (z + i + 1) % 4
            parts[q, i] = dot_nn(lhs(), xs[s, t // 2, t % 2]).astype(BF16)
            remote(parts.at[q, i], remote_dst.at[q, i], send.at[q, i], recv.at[q, i], at_z(i + 1)).start()

        own[q] = dot_nn(lhs(), xs[s, z // 2, z % 2])

    def z_sum(q, s, parts, own, send, recv, remote_dst):
        total = own[q]
        for i in range(3):
            remote(parts.at[q, i], remote_dst.at[q, i], send.at[q, i], recv.at[q, i], at_z(i + 1)).wait_recv()
        for i in range(3):
            total = total + remote_dst[q, i].astype(F32)
        return total

    gu_args = (0, p_gu, o_gu, gu_s, gu_r, r_gu)
    dh_args = (1, p_dh, o_dh, dh_s, dh_r, r_dh)

    def gate_up(q):
        z_loop(q, lambda: wgut[q * 2 * HC:(q + 1) * 2 * HC, :], *gu_args)

    def d_hidden(q):
        z_loop(q, lambda: wd[q * HC:(q + 1) * HC, :], *dh_args)

    def hid_copy(q, i, t):
        piece = hid.at[t, q * HC:(q + 1) * HC]
        return remote(piece, piece, hb_s.at[q, i], hb_r.at[q, i], at_z(i + 1))

    def dgu_copy(q, i, t):
        piece = dgu.at[t, :, q * HC:(q + 1) * HC]
        return remote(piece, piece, dg_s.at[q, i], dg_r.at[q, i], at_z(i + 1))

    def hidden_step(q):
        total = z_sum(q, *gu_args)
        gate, up = total[:HC], total[HC:]
        sig = jax.nn.sigmoid(gate)
        swish = gate * sig
        hid[z, q * HC:(q + 1) * HC] = (swish * up).astype(BF16)
        for i in (1, 0, 2):
            hid_copy(q, i, z).start()
        c_gate[q] = up * sig * (1.0 + gate * (1.0 - sig))
        c_up[q] = swish

    def d_step(q):
        dh = z_sum(q, *dh_args)
        dgu[z, 0, q * HC:(q + 1) * HC] = (dh * c_gate[q]).astype(BF16)
        dgu[z, 1, q * HC:(q + 1) * HC] = (dh * c_up[q]).astype(BF16)
        for i in (1, 0, 2):
            dgu_copy(q, i, z).start()

    def down_copy(q):
        return remote(g_dn.at[q], got_dn.at[q], xd_s.at[q], xd_r.at[q], partner)

    def gu_copy(q):
        return remote(g_gu.at[q], got_gu.at[q], xg_s.at[q], xg_r.at[q], partner)

    def down_local(q):
        return pltpu.make_async_copy(g_dn.at[q], own_dn.at[q], loc_d.at[q])

    def gu_local(q):
        return pltpu.make_async_copy(g_gu.at[q], own_gu.at[q], loc_g.at[q])

    def grad_down(q):
        for i in range(3):
            hid_copy(q, i, (z + 3 - i) % 4).wait_recv()

        @pl.loop(0, 2)
        def _(m):
            feats = pl.ds(pl.multiple_of(m * 640, 640), 640)
            total = None
            for t in range(4):
                part = dot_nt(hid[t, q * HC:(q + 1) * HC], xs[1, t // 2, t % 2, feats])
                total = part if total is None else total + part
            g_dn[q, :, feats] = total.astype(BF16)

        down_copy(q).start()
        down_local(q).start()

    def dgu_wait(q):
        for i in range(3):
            dgu_copy(q, i, (z + 3 - i) % 4).wait_recv()

    def grad_gate_up(q):
        @pl.loop(0, 2)
        def _(m):
            feats = pl.ds(pl.multiple_of(m * 640, 640), 640)
            total = None
            for t in range(4):
                both = jnp.concatenate(
                    [dgu[t, 0, q * HC:(q + 1) * HC], dgu[t, 1, q * HC:(q + 1) * HC]], axis=0
                )
                part = dot_nt(xs[0, t // 2, t % 2, feats], both)
                total = part if total is None else total + part
            g_gu[q, feats, :] = total.astype(BF16)

        gu_copy(q).start()
        gu_local(q).start()

    def sum_sib(s, h):
        there = rows_of(2 * h + 1 - core)
        return remote(o_part.at[s, :, :, there], o_sib.at[s, h], sb_s.at[s, h], sb_r.at[s, h], sibling)

    def sum_terms(s, h, who, product):
        rows = rows_of(2 * h + who)

        @pl.loop(0, 4)
        def _(t):
            o_part[s, t // 2, t % 2, rows, :] = product(rows, t).astype(BF16)

    def sum_start(s, product):
        for h in range(2):
            sum_terms(s, h, 1 - core, product)
            sum_sib(s, h).start()
        for h in range(2):
            sum_terms(s, h, core, product)

    def sum_y(s, d):
        return remote(o_sum.at[s, d], o_y.at[s, d - 1], yr_s.at[s, d - 1], yr_r.at[s, d - 1], at_y(d))

    def sum_cores(s):
        for h in range(2):
            sum_sib(s, h).wait_recv()
        for d in (2, 1, 3, 0):
            yy = (y + d) % 4
            for i in range(2):
                mine = o_part[s, i, yy // 2, rows_of(2 * (yy % 2) + core), :].astype(F32)
                o_sum[s, d, i] = (mine + o_sib[s, yy % 2, i, yy // 2].astype(F32)).astype(BF16)
            if d:
                sum_y(s, d).start()

    def sum_final(s, i):
        return remote(o_fin.at[s, i], o_got.at[s, xh], fn_s.at[s, i], fn_r.at[s, xh], spread_from(i))

    def sum_chips(s):
        for d in (1, 3, 2):
            sum_y(s, d).wait_recv()
        for i in range(2):
            total = o_sum[s, 0, i].astype(F32)
            for d in range(3):
                total = total + o_y[s, d, i].astype(F32)
            o_fin[s, i] = total.astype(BF16)

            @pl.when(jnp.logical_not(home & (xh == i)))
            def _(i=i):
                sum_final(s, i).start()

            @pl.when(home & (xh == i))
            def _(i=i):
                pltpu.make_async_copy(o_fin.at[s, i], o_got.at[s, xh], fn_r.at[s, xh]).start()

    def sum_end(s, result):
        for h in range(2):
            pltpu.make_async_copy(o_fin.at[s, h], o_got.at[s, h], fn_r.at[s, h]).wait()
        result[...] = (o_got[s, 0].astype(F32) + o_got[s, 1].astype(F32)).astype(BF16)

    gate_up(0)
    gate_up(1)
    gather_forward(1)
    hidden_step(0)
    gate_up(2)
    hidden_step(1)
    sib_wait_recv(1)
    grad_down(0)
    gate_up(3)
    d_hidden(0)
    hidden_step(2)
    grad_down(1)
    d_hidden(1)
    hidden_step(3)
    d_step(0)
    grad_down(2)
    d_hidden(2)
    d_step(1)
    d_hidden(3)
    grad_down(3)
    d_step(2)
    dgu_wait(0)
    grad_gate_up(0)
    d_step(3)
    sum_start(0, lambda rows, t: dot_nn(wdt[rows, :], hid[t]))
    dgu_wait(1)
    grad_gate_up(1)
    sum_cores(0)
    dgu_wait(2)
    grad_gate_up(2)
    dgu_wait(3)
    sum_start(1, lambda rows, t: dot_nn(wg[rows, :], dgu[t, 0]) + dot_nn(wu[rows, :], dgu[t, 1]))
    sum_chips(0)
    sum_cores(1)
    grad_gate_up(3)
    sum_end(0, out_t)
    sum_chips(1)
    sum_end(1, dx_t)

    for q in range(NQ):
        for i in range(3):
            remote(p_gu.at[q, i], r_gu.at[q, i], gu_s.at[q, i], gu_r.at[q, i], at_z(i + 1)).wait_send()
            remote(p_dh.at[q, i], r_dh.at[q, i], dh_s.at[q, i], dh_r.at[q, i], at_z(i + 1)).wait_send()
            hid_copy(q, i, z).wait_send()
            dgu_copy(q, i, z).wait_send()
    for s in range(2):
        spread_wait_send(s)
        for d in range(4):
            sib_copy(s, d).wait_send()
        for d in range(1, 4):
            if s == 1:
                y_copy(s, d).wait_send()
            sum_y(s, d).wait_send()
        for i in range(2):
            sum_sib(s, i).wait_send()

            @pl.when(jnp.logical_not(home & (xh == i)))
            def _(s=s, i=i):
                sum_final(s, i).wait_send()

    for q in range(NQ):
        down_local(q).wait()
        gu_local(q).wait()
        down_copy(q).wait()
        gu_copy(q).wait()


def add_kernel(own_gu, got_gu, own_dn, got_dn, gate, up, down):
    total = own_gu[0].astype(F32) + got_gu[0].astype(F32)
    gate[...] = total[:, :HC]
    up[...] = total[:, HC:]
    down[...] = own_dn[0].astype(F32) + got_dn[0].astype(F32)


def body(x_act, grad_out, w_gate, w_up, w_down):
    vmem = pl.BlockSpec(memory_space=pltpu.VMEM)
    hbm = pl.BlockSpec(memory_space=pl.ANY)
    dma = pltpu.SemaphoreType.DMA
    shape = jax.ShapeDtypeStruct

    def buf(*dims, dtype=BF16):
        return pltpu.VMEM(dims, dtype)

    outs = pl.pallas_call(
        layer_kernel,
        out_shape=[
            shape((FEAT, TOK), BF16), shape((FEAT, TOK), BF16),
            shape((NQ, PANEL, 2 * HC), BF16), shape((NQ, PANEL, 2 * HC), BF16),
            shape((NQ, HC, PANEL), BF16), shape((NQ, HC, PANEL), BF16),
        ],
        in_specs=[vmem] * 5,
        out_specs=[vmem, vmem, hbm, hbm, hbm, hbm],
        scratch_shapes=[
            buf(2, 2, 2, PANEL, TOK), buf(2 * HID, PANEL), buf(PANEL, HID),
            buf(NQ, 3, 2 * HC, TOK), buf(NQ, 3, 2 * HC, TOK), buf(NQ, 2 * HC, TOK, dtype=F32),
            buf(NQ, 3, HC, TOK), buf(NQ, 3, HC, TOK), buf(NQ, HC, TOK, dtype=F32),
            buf(NQ, HC, TOK, dtype=F32), buf(NQ, HC, TOK, dtype=F32),
            buf(4, HID, TOK), buf(4, 2, HID, TOK), buf(NQ, PANEL, 2 * HC), buf(NQ, HC, PANEL),
            buf(2, 2, 2, PANEL, TOK), buf(2, 2, 2, 2, FEAT, TOK), buf(2, 4, 2, FEAT, TOK),
            buf(2, 3, 2, FEAT, TOK), buf(2, 2, FEAT, TOK), buf(2, 2, FEAT, TOK),
            dma((2, 2)), dma((2, 2)), dma((2, 3)), dma((2, 3)), dma((2, 4)), dma((2, 4)),
            dma((NQ, 3)), dma((NQ, 3)), dma((NQ, 3)), dma((NQ, 3)),
            dma((NQ, 3)), dma((NQ, 3)), dma((NQ, 3)), dma((NQ, 3)),
            dma((NQ,)), dma((NQ,)), dma((NQ,)), dma((NQ,)), dma((NQ,)), dma((NQ,)),
            dma((2, 2)), dma((2, 2)), dma((2, 3)), dma((2, 3)), dma((2, 2)), dma((2, 2)),
        ],
        name="layer",
        compiler_params=pltpu.CompilerParams(
            collective_id=0, has_side_effects=True, vmem_limit_bytes=60 * 2**20
        ),
    )(x_act[0].T, grad_out[0].T, w_gate, w_up, w_down)
    out_t, dx_t, own_gu, got_gu, own_dn, got_dn = outs

    gu_block = pl.BlockSpec((1, PANEL, 2 * HC), lambda q: (q, 0, 0))
    dn_block = pl.BlockSpec((1, HC, PANEL), lambda q: (q, 0, 0))
    grads = pl.pallas_call(
        add_kernel,
        grid=(NQ,),
        out_shape=[shape((PANEL, HID), F32), shape((PANEL, HID), F32), shape((HID, PANEL), F32)],
        in_specs=[gu_block, gu_block, dn_block, dn_block],
        out_specs=[
            pl.BlockSpec((PANEL, HC), lambda q: (0, q)),
            pl.BlockSpec((PANEL, HC), lambda q: (0, q)),
            pl.BlockSpec((HC, PANEL), lambda q: (q, 0)),
        ],
        name="add_passes",
        compiler_params=pltpu.CompilerParams(vmem_limit_bytes=32 * 2**20),
    )(own_gu, got_gu, own_dn, got_dn)
    return (out_t.T[None], dx_t.T[None], *grads)


def solution(mesh):
    acts = P("branch", "row", "col")
    return jax.shard_map(
        body,
        mesh=mesh,
        in_specs=(acts, acts, P("row", "col"), P("row", "col"), P("col", "row")),
        out_specs=(acts, acts, P("row", "col"), P("row", "col"), P("col", "row")),
        check_vma=False,
    )
```

time: 752 us -> 185 us (0.25)
  waiting for transfers between devices: 597 us -> 0 us
  Pallas kernels: 0 us -> 174 us
  local copies, waits for them, and re-layouts: 82.7 us -> 7.44 us
  matrix products: 41 us -> 0 us
  between operations: 14.2 us -> 0.66 us
  other arithmetic: 12.8 us -> 0 us
    all_gather x7 -> x0, waiting for transfers between devices: 314 us -> none  [the longest x1 103 us: body(): panels = lax.all_gather(stacked, 'row', axis=1, tiled=True)]
    reduce_scatter x4 -> x0, waiting for transfers between devices: 216 us -> none  [the longest x1 76.7 us: body(): lax.psum_scatter(dx_terms.astype(jnp.bfloat16), 'col', scatter_dimension=...]
    pallas_call x0 -> x2, Pallas kernels: none -> 174 us  [the longest x1 171 us: body(): pl.pallas_call(layer_kernel, out_shape=[shape((FEAT, TOK), BF16), shape((...]
    unnamed x13 -> x0, waiting for transfers between devices: 66.9 us -> none
    convert_element_type x5 -> x0, local copies, waits for them, and re-layouts: 64.7 us -> none  [the longest x2 26.2 us: body(): up_term.astype(jnp.bfloat16)]
    dot_general x9 -> x0, matrix products: 41 us -> none  [the longest x3 15 us: contract_cols(): lax.dot_general(left, right, (((1,), (1,)), ((), ())), preferred_element_...]
    unnamed x8 -> x14, local copies, waits for them, and re-layouts: 18 us -> 7.44 us
    convert_element_type x3 -> x0, other arithmetic: 9.34 us -> none  [the longest x1 3.17 us: body(): lax.all_gather(part_gate.astype(jnp.bfloat16), 'branch', axis=0, tiled=True)]
  transfers between devices with their start and end apart: 12 -> 0, of which waited for: 11 -> 0; matrix products, arithmetic and copies ran while one was open for 13% -> 0% of each run, Pallas kernels for 0% -> 0%
where the time goes in v1:
time: 185 us; the launch traced here: 182 us
  Pallas kernels  174 us (94%)
  local copies, waits for them, and re-layouts  7.44 us (4%)
    pallas_call x1, Pallas kernels, body(): pl.pallas_call(layer_kernel, out_shape=[shape((FEAT, TOK), BF16), shape((...  171 us
    unnamed x14, local copies, waits for them, and re-layouts  7.44 us

profile of v1, /device:TPU:66, one launch (start us, length us, event | category | flops | bytes accessed | tf_op | source)
XLA Modules:
  0.0 182.1 jit_solution(6106460855736103128)
XLA Ops:
  0.6 170.6 %layer.1 = (bf16[320,256]{1,0:T(8,128)(2,1)}, bf16[320,256]{1,0:T(8,128)(2,1)}, bf16[4,1280,256]{2,1,0:T(8,128)(2,1)}, bf16[4,1280,256]{2,1,0:T(8,128)(2,1)}, bf...) custom-call(bf16[320,256]{1,0:T(8,128)(2,1)} %bitcast.12, bf16[320,256]{1,0:T(8,128)(2,1)} %bitcast.13, ...), custom_call_target="tpu_custom_call" | custom-call | tf_op jit(solution)/shard_map/layer/pallas_call | solution.py:409
  171.2 0.0 copy-start
  171.2 1.7 copy-done
  173.0 0.0 copy-start.1
  173.0 1.7 copy-done.1
  174.7 0.0 copy-start.2
  174.7 1.3 copy-done.2
  176.0 0.0 copy-start.3
  176.0 1.3 copy-done.3
  177.3 0.0 copy-start.5
  177.3 0.0 copy-start.4
  177.3 3.4 %add_passes.1 = (f32[1280,512]{1,0:T(8,128)}, f32[1280,512]{1,0:T(8,128)}, f32[512,1280]{1,0:T(8,128)}) custom-call(bf16[4,1280,256]{2,1,0:T(8,128)(2,1)S(1)} %copy-done, bf16[4,1280,256]{2,1,0:T(8,128)(2,1)S(1)} %copy-done.1, bf16[4,128,1280]{2,1,0:T(8,128)(2,1)S(1)} %copy-done.2, bf16[4,128,1280]{2,1,0:T(8,128)(2,1)S(1)} %copy-done.3), custom_call_target="tpu_custom_call" | custom-call | tf_op jit(solution)/shard_map/add_passes/pallas_call | solution.py:441
  180.7 0.0 copy-done.5
  180.7 0.7 copy.12
  181.4 0.0 copy-done.4
  181.4 0.7 copy.13
Async XLA Ops:
  171.2 1.7 copy-start
  173.0 1.7 copy-start.1
  174.7 1.3 copy-start.2
  176.0 1.3 copy-start.3
  177.3 3.4 %copy-start.5 = (bf16[320,256]{1,0:T(8,128)(2,1)S(1)}, bf16[320,256]{1,0:T(8,128)(2,1)}, u32[]{:S(2)}) copy-start(bf16[320,256]{1,0:T(8,128)(2,1)} %get-tuple-element.14) | copy-start | bytes 491524
  177.3 4.1 %copy-start.4 = (bf16[320,256]{1,0:T(8,128)(2,1)S(1)}, bf16[320,256]{1,0:T(8,128)(2,1)}, u32[]{:S(2)}) copy-start(bf16[320,256]{1,0:T(8,128)(2,1)} %get-tuple-element.15) | copy-start | bytes 491524

commit v2 on v1

v2 whole, which is shorter than its diff:
```python
import functools

import jax
import jax.numpy as jnp
from jax import lax
from jax.experimental import pallas as pl
from jax.experimental.pallas import tpu as pltpu
from jax.sharding import PartitionSpec as P

MESH = pl.DeviceIdType.MESH
BF16 = jnp.bfloat16
F32 = jnp.float32

N_ROW = 4
FEAT = 320
TOK = 256
PANEL = 1280
HID = 512
NQ = 4
HC = HID // NQ


def dot_nn(left, right):
    return jnp.dot(left, right, preferred_element_type=F32)


def dot_nt(left, right):
    return lax.dot_general(left, right, (((1,), (1,)), ((), ())), preferred_element_type=F32)


def flip(a, b):
    return a + b - 2 * a * b


def layer_kernel(
    x_in, dy_in, wg_in, wu_in, wd_in,
    o_got, all_gu, all_dn,
    xs, wg, wu, wd, wgut, wdt,
    p_gu, t_gu, r_gu, o_gu, p_dh, t_dh, r_dh, o_dh, c_gate, c_up,
    hid, dgu, g_gu, g_dn, x_gu, x_dn,
    o_part, o_sib, o_sum, o_y, o_fin,
    w_r, wf_s, wf_r,
    p0_s, p0_r, p1_s, p1_r, p2_s, p2_r,
    gu_s, gu_r, hb_s, hb_r, dh_s, dh_r, dg_s, dg_r,
    xd_s, xd_r, xg_s, xg_r, loc_d, loc_g,
    sb_s, sb_r, yr_s, yr_r, fn_s, fn_r,
):
    b, z, c = lax.axis_index("branch"), lax.axis_index("row"), lax.axis_index("col")
    y, xh, sub, core = (c // 2) % 4, c // 8, c % 4, c % 2
    yh = y // 2
    zh, zl = z // 2, z % 2
    low = flip(yh, zl)

    def at_z(d):
        return (b, (z + d) % N_ROW, c)

    def at_y(d):
        return (b, z, xh * 8 + ((y + d) % 4) * 2 + core)

    sibling = (b, z, c + 1 - 2 * core)
    partner = (1 - b, z, c)
    other = (1 - b, z, (c + 8) % 16)

    def spread_to(h):
        return (b, c // 4, h * 8 + low * 4 + sub)

    def spread_from(i):
        return (b, 2 * i + low, 4 * z + sub)

    def to_self(h):
        return (c // 4 == z) & (xh == h) & (low == yh)

    def from_self(i):
        return (c // 4 == z) & (2 * i + low == z)

    def rows_of(j):
        return pl.ds(pl.multiple_of(j * FEAT, 64), FEAT)

    def remote(src, dst, ssem, rsem, to):
        return pltpu.make_async_remote_copy(
            src_ref=src, dst_ref=dst, send_sem=ssem, recv_sem=rsem, device_id=to, device_id_type=MESH
        )

    def weight_pair(i, n):
        part = pl.ds(pl.multiple_of(b * (HID // 2) + i * HC, HC), HC)
        mine, theirs = pl.ds((2 * i + 1) * HC, HC), pl.ds(2 * i * HC, HC)
        if n == 2:
            return wd_in.at[part], wd.at[mine], wd.at[theirs]
        src, dst = ((wg_in, wg), (wu_in, wu))[n]
        return src.at[:, part], dst.at[:, mine], dst.at[:, theirs]

    def weight_local(i, n):
        src, mine, _ = weight_pair(i, n)
        return pltpu.make_async_copy(src, mine, w_r.at[i, n])

    def weight_copy(i, n):
        src, _, theirs = weight_pair(i, n)
        return remote(src, theirs, wf_s.at[i, n], wf_r.at[i, n], other)

    for i in range(2):
        for n in range(3):
            weight_local(i, n).start()

    barrier = pltpu.get_barrier_semaphore()
    for to in [at_z(1), at_z(2), at_z(3), at_y(1), at_y(2), at_y(3), sibling, partner, other]:
        pl.semaphore_signal(barrier, inc=1, device_id=to, device_id_type=MESH)
    for i in range(2):
        @pl.when(jnp.logical_not(to_self(i)))
        def _(i=i):
            pl.semaphore_signal(barrier, inc=1, device_id=spread_to(i), device_id_type=MESH)

        @pl.when(jnp.logical_not(from_self(i)))
        def _(i=i):
            pl.semaphore_signal(barrier, inc=1, device_id=spread_from(i), device_id_type=MESH)

    stay = (c // 4 == z) & (low == yh)
    pl.semaphore_wait(barrier, jnp.where(stay, 11, 13))

    acts = (x_in, dy_in)

    def spread_copy(s, h):
        return remote(
            acts[s], xs.at[s, zh, zl, rows_of(sub)], p0_s.at[s, h], p0_r.at[s, zh], spread_to(h)
        )

    def spread_local(s):
        return pltpu.make_async_copy(
            acts[s], xs.at[s, zh, zl, rows_of(sub)], p0_r.at[s, zh]
        )

    def spread_start(s):
        for h in range(2):
            @pl.when(jnp.logical_not(to_self(h)))
            def _(h=h):
                spread_copy(s, h).start()

            @pl.when(to_self(h))
            def _():
                spread_local(s).start()

    def spread_wait_recv(s):
        for i in range(2):
            pltpu.make_async_copy(
                acts[s], xs.at[s, i, low, rows_of(sub)], p0_r.at[s, i]
            ).wait()

    def spread_wait_send(s):
        for h in range(2):
            @pl.when(jnp.logical_not(to_self(h)))
            def _(h=h):
                spread_copy(s, h).wait_send()

    def block(s, i, yy, k):
        return xs.at[s, i, flip(yy // 2, zl), rows_of(2 * (yy % 2) + k)]

    def group(s, d, k):
        yy = (y - d + 4) % 4
        return xs.at[s, :, flip(yy // 2, zl), rows_of(2 * (yy % 2) + k)]

    def y_copy(s, slot):
        if slot < 2:
            piece = group(s, 0, core)
        else:
            piece = block(s, slot - 2, (y + (3 if slot == 2 else 1)) % 4, core)
        to = at_y(1 if slot % 2 == 0 else 3)
        return remote(piece, piece, p1_s.at[s, slot], p1_r.at[s, slot], to)

    def y_wait_recv(s, slot):
        if slot < 2:
            piece = group(s, 1 if slot == 0 else 3, core)
        else:
            piece = block(s, slot - 2, (y + 2) % 4, core)
        remote(piece, piece, p1_s.at[s, slot], p1_r.at[s, slot], at_y(1)).wait_recv()

    def sib_copy(s, d):
        piece = group(s, d, core)
        return remote(piece, piece, p2_s.at[s, d], p2_r.at[s, d], sibling)

    def sib_wait_recv(s):
        for d in range(4):
            there = group(s, d, 1 - core)
            remote(there, there, p2_s.at[s, d], p2_r.at[s, d], sibling).wait_recv()

    def gather_start(s):
        y_copy(s, 0).start()
        y_copy(s, 1).start()
        sib_copy(s, 0).start()

    def gather_pass(s):
        y_wait_recv(s, 0)
        y_copy(s, 2).start()
        y_wait_recv(s, 1)
        y_copy(s, 3).start()
        sib_copy(s, 1).start()
        sib_copy(s, 3).start()

    def gather_last(s):
        y_wait_recv(s, 2)
        y_wait_recv(s, 3)
        sib_copy(s, 2).start()

    spread_start(0)

    for i, n in ((0, 0), (0, 1), (1, 0), (1, 1), (0, 2), (1, 2)):
        weight_copy(i, n).start()

    def turn(q):
        cols = pl.ds(q * HC, HC)
        wgut[q * 2 * HC:q * 2 * HC + HC, :] = wg[:, cols].T
        wgut[q * 2 * HC + HC:(q + 1) * 2 * HC, :] = wu[:, cols].T

    def turn_other(i):
        weight_copy(i, 0).wait_recv()
        weight_copy(i, 1).wait_recv()
        turn(2 * i)

    def turn_down():
        @pl.loop(0, NQ)
        def _(q):
            cols = pl.ds(pl.multiple_of(q * HC, HC), HC)
            wdt[:, cols] = wd[cols, :].T

    for i in range(2):
        for n in range(3):
            weight_local(i, n).wait()
        turn(2 * i + 1)

    spread_wait_recv(0)
    gather_start(0)
    spread_start(1)
    gather_pass(0)
    spread_wait_recv(1)
    gather_start(1)
    turn_other(0)
    gather_last(0)
    sib_wait_recv(0)

    def term_copy(flow, q, slot):
        _, parts, far, near, _, send, recv, half = flow
        rows = pl.ds((0, half, half, 0, 0, half)[slot], half)
        src = parts.at[q, (1, 1, 0, 2, 0, 2)[slot], rows]
        dst = far.at[q, slot] if slot < 2 else near.at[q, slot % 2, rows]
        return remote(src, dst, send.at[q, slot], recv.at[q, slot], at_z(3 if slot % 2 else 1))

    def terms(flow, q, lhs):
        s, parts, _, _, own, _, _, _ = flow
        for d in (2, 1, 3, 0):
            t = (z + d) % 4
            term = dot_nn(lhs, xs[s, t // 2, t % 2])
            if d == 0:
                own[q] = term
                continue
            parts[q, d - 1] = term.astype(BF16)
            for slot in {2: (0, 1), 1: (2,), 3: (3,)}[d]:
                term_copy(flow, q, slot).start()

    def relay(flow, q):
        _, parts, far, _, _, _, _, half = flow
        for slot in (0, 1):
            rows = pl.ds(slot * half, half)
            term_copy(flow, q, slot).wait_recv()
            parts[q, 2 * slot, rows, :] = (
                parts[q, 2 * slot, rows, :].astype(F32) + far[q, slot].astype(F32)
            ).astype(BF16)
            term_copy(flow, q, slot + 4).start()

    def total(flow, q):
        _, _, _, near, own, _, _, _ = flow
        for slot in (2, 3, 4, 5):
            term_copy(flow, q, slot).wait_recv()
        return own[q] + near[q, 0].astype(F32) + near[q, 1].astype(F32)

    gu_flow = (0, p_gu, t_gu, r_gu, o_gu, gu_s, gu_r, HC)
    dh_flow = (1, p_dh, t_dh, r_dh, o_dh, dh_s, dh_r, HC // 2)

    def gate_up(q):
        terms(gu_flow, q, wgut[q * 2 * HC:(q + 1) * 2 * HC, :])

    def d_hidden(q):
        terms(dh_flow, q, wd[q * HC:(q + 1) * HC, :])

    def hid_piece(q, t, half):
        if half is None:
            return hid.at[t, q * HC:(q + 1) * HC]
        return hid.at[t, q * HC + half * (HC // 2):q * HC + (half + 1) * (HC // 2)]

    def dgu_piece(q, t, half):
        rows = pl.ds(q * HC, HC)
        return dgu.at[t, :, rows] if half is None else dgu.at[t, half, rows]

    def block_copy(piece, q, slot, send, recv, step):
        part = piece(q, (z + (step, -step)[slot % 2] + 4) % 4, None if slot < 2 else slot - 2)
        return remote(part, part, send.at[q, slot], recv.at[q, slot], at_z(3 if slot % 2 else 1))

    def send_copy(flow, q, slot):
        piece, send, recv = flow
        return block_copy(piece, q, slot, send, recv, 0 if slot < 2 else 3)

    def recv_copy(flow, q, slot):
        piece, send, recv = flow
        return block_copy(piece, q, slot, send, recv, 3 if slot < 2 else 2)

    def blocks_start(flow, q):
        for slot in (0, 1):
            send_copy(flow, q, slot).start()

    def blocks_pass(flow, q):
        for slot in (0, 1):
            recv_copy(flow, q, slot).wait_recv()
            send_copy(flow, q, slot + 2).start()

    def blocks_wait(flow, q):
        for slot in (2, 3):
            recv_copy(flow, q, slot).wait_recv()

    hid_flow = (hid_piece, hb_s, hb_r)
    dgu_flow = (dgu_piece, dg_s, dg_r)

    def hidden_step(q):
        both = total(gu_flow, q)
        gate, up = both[:HC], both[HC:]
        sig = jax.nn.sigmoid(gate)
        swish = gate * sig
        hid[z, q * HC:(q + 1) * HC] = (swish * up).astype(BF16)
        blocks_start(hid_flow, q)
        c_gate[q] = up * sig * (1.0 + gate * (1.0 - sig))
        c_up[q] = swish

    def d_step(q):
        dh = total(dh_flow, q)
        dgu[z, 0, q * HC:(q + 1) * HC] = (dh * c_gate[q]).astype(BF16)
        dgu[z, 1, q * HC:(q + 1) * HC] = (dh * c_up[q]).astype(BF16)
        blocks_start(dgu_flow, q)

    def pass_copy(mine, theirs, full, send, recv, q):
        if q % 2 == 0:
            return remote(mine.at[q], theirs.at[q // 2], send.at[q], recv.at[q], other)
        return remote(mine.at[q], full.at[2 * b + q // 2], send.at[q], recv.at[q], partner)

    def down_copy(q):
        return pass_copy(g_dn, x_dn, all_dn, xd_s, xd_r, q)

    def gu_copy(q):
        return pass_copy(g_gu, x_gu, all_gu, xg_s, xg_r, q)

    def down_local(q):
        return pltpu.make_async_copy(g_dn.at[q], all_dn.at[2 * b + q // 2], loc_d.at[q // 2])

    def gu_local(q):
        return pltpu.make_async_copy(g_gu.at[q], all_gu.at[2 * b + q // 2], loc_g.at[q // 2])

    def grad_down(q):
        if q % 2:
            down_copy(q - 1).wait_recv()

        @pl.loop(0, 2)
        def _(m):
            feats = pl.ds(pl.multiple_of(m * 640, 640), 640)
            acc = None
            for t in range(4):
                part = dot_nt(hid[t, q * HC:(q + 1) * HC], xs[1, t // 2, t % 2, feats])
                acc = part if acc is None else acc + part
            if q % 2:
                acc = acc + x_dn[q // 2, :, feats].astype(F32)
            g_dn[q, :, feats] = acc.astype(BF16)

        down_copy(q).start()
        if q % 2:
            down_local(q).start()

    def grad_gate_up(q):
        if q % 2:
            gu_copy(q - 1).wait_recv()

        @pl.loop(0, 2)
        def _(m):
            feats = pl.ds(pl.multiple_of(m * 640, 640), 640)
            acc = None
            for t in range(4):
                both = jnp.concatenate(
                    [dgu[t, 0, q * HC:(q + 1) * HC], dgu[t, 1, q * HC:(q + 1) * HC]], axis=0
                )
                part = dot_nt(xs[0, t // 2, t % 2, feats], both)
                acc = part if acc is None else acc + part
            if q % 2:
                acc = acc + x_gu[q // 2, feats, :].astype(F32)
            g_gu[q, feats, :] = acc.astype(BF16)

        gu_copy(q).start()
        if q % 2:
            gu_local(q).start()

    def sum_sib(s, h):
        there = rows_of(2 * h + 1 - core)
        return remote(o_part.at[s, :, :, there], o_sib.at[s, h], sb_s.at[s, h], sb_r.at[s, h], sibling)

    def sum_terms(s, h, who, product):
        rows = rows_of(2 * h + who)

        @pl.loop(0, 4)
        def _(t):
            o_part[s, t // 2, t % 2, rows, :] = product(rows, t).astype(BF16)

    def sum_start(s, product):
        for h in range(2):
            sum_terms(s, h, 1 - core, product)
            sum_sib(s, h).start()
        for h in range(2):
            sum_terms(s, h, core, product)

    def sum_y(s, d):
        return remote(o_sum.at[s, d], o_y.at[s, d - 1], yr_s.at[s, d - 1], yr_r.at[s, d - 1], at_y(d))

    def sum_cores(s):
        for h in range(2):
            sum_sib(s, h).wait_recv()
        for d in (2, 1, 3, 0):
            yy = (y + d) % 4
            for i in range(2):
                mine = o_part[s, i, flip(yy // 2, zl), rows_of(2 * (yy % 2) + core), :].astype(F32)
                o_sum[s, d, i] = (mine + o_sib[s, yy % 2, i, flip(yy // 2, zl)].astype(F32)).astype(BF16)
            if d:
                sum_y(s, d).start()

    def sum_final(s, i):
        return remote(o_fin.at[s, i], o_got.at[s, xh], fn_s.at[s, i], fn_r.at[s, xh], spread_from(i))

    def sum_chips(s):
        for d in (1, 3, 2):
            sum_y(s, d).wait_recv()
        for i in range(2):
            total = o_sum[s, 0, i].astype(F32)
            for d in range(3):
                total = total + o_y[s, d, i].astype(F32)
            o_fin[s, i] = total.astype(BF16)

            @pl.when(jnp.logical_not(from_self(i)))
            def _(i=i):
                sum_final(s, i).start()

            @pl.when(from_self(i))
            def _(i=i):
                pltpu.make_async_copy(o_fin.at[s, i], o_got.at[s, xh], fn_r.at[s, xh]).start()

    def sum_end(s):
        for h in range(2):
            pltpu.make_async_copy(o_fin.at[s, h], o_got.at[s, h], fn_r.at[s, h]).wait()

    gate_up(0)
    gate_up(1)
    gather_pass(1)
    relay(gu_flow, 0)
    turn_other(1)
    gate_up(2)
    relay(gu_flow, 1)
    hidden_step(0)
    gather_last(1)
    gate_up(3)
    relay(gu_flow, 2)
    hidden_step(1)
    blocks_pass(hid_flow, 0)
    sib_wait_recv(1)
    weight_copy(0, 2).wait_recv()
    d_hidden(0)
    relay(gu_flow, 3)
    hidden_step(2)
    blocks_pass(hid_flow, 1)
    blocks_wait(hid_flow, 0)
    grad_down(0)
    weight_copy(1, 2).wait_recv()
    hidden_step(3)
    blocks_pass(hid_flow, 2)
    d_hidden(1)
    relay(dh_flow, 0)
    blocks_wait(hid_flow, 2)
    grad_down(2)
    blocks_pass(hid_flow, 3)
    d_hidden(2)
    relay(dh_flow, 1)
    d_step(0)
    blocks_wait(hid_flow, 1)
    grad_down(1)
    blocks_wait(hid_flow, 3)
    turn_down()
    sum_start(0, lambda rows, t: dot_nn(wdt[rows, :], hid[t]))
    d_hidden(3)
    relay(dh_flow, 2)
    d_step(1)
    blocks_pass(dgu_flow, 0)
    grad_down(3)
    sum_cores(0)
    relay(dh_flow, 3)
    d_step(2)
    blocks_pass(dgu_flow, 1)
    blocks_wait(dgu_flow, 0)
    grad_gate_up(0)
    d_step(3)
    blocks_pass(dgu_flow, 2)
    sum_chips(0)
    blocks_wait(dgu_flow, 2)
    grad_gate_up(2)
    blocks_pass(dgu_flow, 3)
    blocks_wait(dgu_flow, 1)
    blocks_wait(dgu_flow, 3)
    sum_start(1, lambda rows, t: dot_nn(wg[rows, :], dgu[t, 0]) + dot_nn(wu[rows, :], dgu[t, 1]))
    grad_gate_up(1)
    sum_cores(1)
    grad_gate_up(3)
    sum_chips(1)
    sum_end(0)
    sum_end(1)

    for q in range(NQ):
        for slot in range(6):
            term_copy(gu_flow, q, slot).wait_send()
            term_copy(dh_flow, q, slot).wait_send()
        for slot in range(4):
            send_copy(hid_flow, q, slot).wait_send()
            send_copy(dgu_flow, q, slot).wait_send()
    for s in range(2):
        spread_wait_send(s)
        for d in range(4):
            sib_copy(s, d).wait_send()
            y_copy(s, d).wait_send()
        for d in range(1, 4):
            sum_y(s, d).wait_send()
        for i in range(2):
            sum_sib(s, i).wait_send()

            @pl.when(jnp.logical_not(from_self(i)))
            def _(s=s, i=i):
                sum_final(s, i).wait_send()

    for q in range(NQ):
        down_copy(q).wait_send()
        gu_copy(q).wait_send()
        if q % 2:
            down_local(q).wait()
            gu_local(q).wait()
            down_landed = all_dn.at[2 * (1 - b) + q // 2]
            gu_landed = all_gu.at[2 * (1 - b) + q // 2]
            remote(g_dn.at[q], down_landed, xd_s.at[q], xd_r.at[q], partner).wait_recv()
            remote(g_gu.at[q], gu_landed, xg_s.at[q], xg_r.at[q], partner).wait_recv()
    for i in range(2):
        for n in range(3):
            weight_copy(i, n).wait_send()


def widen_kernel(all_gu, all_dn, got, gate, up, down, out_t, dx_t):
    gate[...] = all_gu[0, :, :HC].astype(F32)
    up[...] = all_gu[0, :, HC:].astype(F32)
    down[...] = all_dn[0].astype(F32)

    @pl.when(pl.program_id(0) == 0)
    def _():
        out_t[...] = (got[0, 0].astype(F32) + got[0, 1].astype(F32)).astype(BF16)
        dx_t[...] = (got[1, 0].astype(F32) + got[1, 1].astype(F32)).astype(BF16)


def body(x_act, grad_out, w_gate, w_up, w_down):
    hbm = pl.BlockSpec(memory_space=pl.ANY)
    dma = pltpu.SemaphoreType.DMA
    shape = jax.ShapeDtypeStruct

    def buf(*dims, dtype=BF16):
        return pltpu.VMEM(dims, dtype)

    outs = pl.pallas_call(
        layer_kernel,
        out_shape=[
            shape((2, 2, FEAT, TOK), BF16),
            shape((NQ, PANEL, 2 * HC), BF16), shape((NQ, HC, PANEL), BF16),
        ],
        in_specs=[hbm] * 5,
        out_specs=[hbm] * 3,
        scratch_shapes=[
            buf(2, 2, 2, PANEL, TOK), buf(PANEL, HID), buf(PANEL, HID), buf(HID, PANEL),
            buf(2 * HID, PANEL), buf(PANEL, HID),
            buf(NQ, 3, 2 * HC, TOK), buf(NQ, 2, HC, TOK), buf(NQ, 2, 2 * HC, TOK),
            buf(NQ, 2 * HC, TOK, dtype=F32),
            buf(NQ, 3, HC, TOK), buf(NQ, 2, HC // 2, TOK), buf(NQ, 2, HC, TOK),
            buf(NQ, HC, TOK, dtype=F32),
            buf(NQ, HC, TOK, dtype=F32), buf(NQ, HC, TOK, dtype=F32),
            buf(4, HID, TOK), buf(4, 2, HID, TOK), buf(NQ, PANEL, 2 * HC), buf(NQ, HC, PANEL),
            buf(2, PANEL, 2 * HC), buf(2, HC, PANEL),
            buf(2, 2, 2, PANEL, TOK), buf(2, 2, 2, 2, FEAT, TOK), buf(2, 4, 2, FEAT, TOK),
            buf(2, 3, 2, FEAT, TOK), buf(2, 2, FEAT, TOK),
            dma((2, 3)), dma((2, 3)), dma((2, 3)),
            dma((2, 2)), dma((2, 2)), dma((2, 4)), dma((2, 4)), dma((2, 4)), dma((2, 4)),
            dma((NQ, 6)), dma((NQ, 6)), dma((NQ, 4)), dma((NQ, 4)),
            dma((NQ, 6)), dma((NQ, 6)), dma((NQ, 4)), dma((NQ, 4)),
            dma((NQ,)), dma((NQ,)), dma((NQ,)), dma((NQ,)), dma((2,)), dma((2,)),
            dma((2, 2)), dma((2, 2)), dma((2, 3)), dma((2, 3)), dma((2, 2)), dma((2, 2)),
        ],
        name="layer",
        compiler_params=pltpu.CompilerParams(
            collective_id=0, has_side_effects=True, vmem_limit_bytes=60 * 2**20
        ),
    )(x_act[0].T, grad_out[0].T, w_gate, w_up, w_down)
    got, all_gu, all_dn = outs

    gu_block = pl.BlockSpec((1, PANEL, 2 * HC), lambda q: (q, 0, 0))
    dn_block = pl.BlockSpec((1, HC, PANEL), lambda q: (q, 0, 0))
    whole = pl.BlockSpec((FEAT, TOK), lambda q: (0, 0))
    *grads, out_t, dx_t = pl.pallas_call(
        widen_kernel,
        grid=(NQ,),
        out_shape=[
            shape((PANEL, HID), F32), shape((PANEL, HID), F32), shape((HID, PANEL), F32),
            shape((FEAT, TOK), BF16), shape((FEAT, TOK), BF16),
        ],
        in_specs=[
            gu_block, dn_block,
            pl.BlockSpec((2, 2, FEAT, TOK), lambda q: (0, 0, 0, 0)),
        ],
        out_specs=[
            pl.BlockSpec((PANEL, HC), lambda q: (0, q)),
            pl.BlockSpec((PANEL, HC), lambda q: (0, q)),
            pl.BlockSpec((HC, PANEL), lambda q: (q, 0)),
            whole, whole,
        ],
        name="widen",
        compiler_params=pltpu.CompilerParams(vmem_limit_bytes=60 * 2**20),
    )(all_gu, all_dn, got)
    return (out_t.T[None], dx_t.T[None], *grads)


def solution(mesh):
    acts = P("branch", "row", "col")
    return jax.shard_map(
        body,
        mesh=mesh,
        in_specs=(acts, acts, P("row", "col"), P("row", "col"), P("col", "row")),
        out_specs=(acts, acts, P("row", "col"), P("row", "col"), P("col", "row")),
        check_vma=False,
    )
```

time: 185 us -> 162 us (0.88); the launches traced: 182 us -> 161 us
  Pallas kernels: 174 us -> 161 us
  local copies, waits for them, and re-layouts: 7.44 us -> 0 us
    pallas_call x2, Pallas kernels: 174 us -> 161 us  [the longest x1 155 us: body(): pl.pallas_call(layer_kernel, out_shape=[shape((2, 2, FEAT, TOK), BF16), s...]
    unnamed x14 -> x0, local copies, waits for them, and re-layouts: 7.44 us -> none
where the time goes in v2:
time: 162 us; the launch traced here: 161 us
  Pallas kernels  161 us (99%)
    pallas_call x1, Pallas kernels, body(): pl.pallas_call(layer_kernel, out_shape=[shape((2, 2, FEAT, TOK), BF16), s...  155 us
    pallas_call x1, Pallas kernels, body(): pl.pallas_call(widen_kernel, grid=(NQ,), out_shape=[shape((PANEL, HID), F...  6.07 us

profile of v2, /device:TPU:66, one launch (start us, length us, event | category | flops | bytes accessed | tf_op | source)
XLA Modules:
  0.0 161.5 jit_solution(8998882621235744616)
XLA Ops:
  0.6 154.6 %layer.1 = (bf16[2,2,320,256]{3,2,1,0:T(8,128)(2,1)}, bf16[4,1280,256]{2,1,0:T(8,128)(2,1)}, bf16[4,128,1280]{2,1,0:T(8,128)(2,1)}) custom-call(bf16[320,256]{1,0:T(8,128)(2,1)} %bitcast.12, bf16[320,256]{1,0:T(8,128)(2,1)} %bitcast.13, bf16[1280,512]{1,0:T(8,128)(2,1)} %wg_in.1, bf16[1280,512]{1,0:T(8,128)(2,1)} %wu_in.1, bf16[512,1280]{1,0:T(8,128)(2,1)} %wd_in.1), custom_call_target="tpu_custom_call" | custom-call | tf_op jit(solution)/shard_map/layer/pallas_call | solution.py:568
  155.3 6.1 %widen.1 = (f32[1280,512]{1,0:T(8,128)}, f32[1280,512]{1,0:T(8,128)}, f32[512,1280]{1,0:T(8,128)}, bf16[320,256]{1,0:T(8,128)(2,1)}, bf16[320,256]{1,0:T(8,128)(2,1)}) custom-call(bf16[4,1280,256]{2,1,0:T(8,128)(2,1)} %get-tuple-element.13.all_gu, bf16[4,128,1280]{2,1,0:T(8,128)(2,1)} %get-tuple-element.14.all_dn, bf16[2,2,320,256]{3,2,1,0:T(8,128)(2,1)} %get-tuple-element.15.got), custom_call_target="tpu_custom_call" | custom-call | tf_op jit(solution)/shard_map/widen/pallas_call | solution.py:605

commit v3 on v2

--- a/solution.py
+++ b/solution.py
@@ -38,12 +38,12 @@
     xs, wg, wu, wd, wgut, wdt,
     p_gu, t_gu, r_gu, o_gu, p_dh, t_dh, r_dh, o_dh, c_gate, c_up,
     hid, dgu, g_gu, g_dn, x_gu, x_dn,
-    o_part, o_sib, o_sum, o_y, o_fin,
+    o_part, o_sib, o_sum, o_y, o_fin, o_mid,
     w_r, wf_s, wf_r,
     p0_s, p0_r, p1_s, p1_r, p2_s, p2_r,
     gu_s, gu_r, hb_s, hb_r, dh_s, dh_r, dg_s, dg_r,
     xd_s, xd_r, xg_s, xg_r, loc_d, loc_g,
-    sb_s, sb_r, yr_s, yr_r, fn_s, fn_r,
+    sb_s, sb_r, yr_s, yr_r, md_s, md_r, fn_s, fn_r,
 ):
     b, z, c = lax.axis_index("branch"), lax.axis_index("row"), lax.axis_index("col")
     y, xh, sub, core = (c // 2) % 4, c // 8, c % 4, c % 2
@@ -69,6 +69,15 @@
 
     def to_self(h):
         return (c // 4 == z) & (xh == h) & (low == yh)
+
+    def in_plane(h):
+        return (b, z, h * 8 + low * 4 + sub)
+
+    def same_place(h):
+        return (xh == h) & (low == yh)
+
+    def same_row(i):
+        return 2 * i + low == z
 
     def from_self(i):
         return (c // 4 == z) & (2 * i + low == z)
@@ -113,8 +122,12 @@
         def _(i=i):
             pl.semaphore_signal(barrier, inc=1, device_id=spread_from(i), device_id_type=MESH)
 
+        @pl.when(jnp.logical_not(same_place(i)))
+        def _(i=i):
+            pl.semaphore_signal(barrier, inc=1, device_id=in_plane(i), device_id_type=MESH)
+
     stay = (c // 4 == z) & (low == yh)
-    pl.semaphore_wait(barrier, jnp.where(stay, 11, 13))
+    pl.semaphore_wait(barrier, jnp.where(stay, 11, 13) + jnp.where(low == yh, 1, 2))
 
     acts = (x_in, dy_in)
 
@@ -332,16 +345,21 @@
         dgu[z, 1, q * HC:(q + 1) * HC] = (dh * c_up[q]).astype(BF16)
         blocks_start(dgu_flow, q)
 
-    def pass_copy(mine, theirs, full, send, recv, q):
+    def pass_copy(mine, theirs, full, send, recv, q, m, part):
         if q % 2 == 0:
-            return remote(mine.at[q], theirs.at[q // 2], send.at[q], recv.at[q], other)
-        return remote(mine.at[q], full.at[2 * b + q // 2], send.at[q], recv.at[q], partner)
-
-    def down_copy(q):
-        return pass_copy(g_dn, x_dn, all_dn, xd_s, xd_r, q)
-
-    def gu_copy(q):
-        return pass_copy(g_gu, x_gu, all_gu, xg_s, xg_r, q)
+            to, dst = other, theirs.at[q // 2]
+        else:
+            to, dst = partner, full.at[2 * b + q // 2]
+        return remote(mine.at[q].at[part], dst.at[part], send.at[q, m], recv.at[q, m], to)
+
+    def feats_of(m):
+        return pl.ds(pl.multiple_of(m * (PANEL // 2), PANEL // 2), PANEL // 2)
+
+    def down_copy(q, m):
+        return pass_copy(g_dn, x_dn, all_dn, xd_s, xd_r, q, m, (slice(None), feats_of(m)))
+
+    def gu_copy(q, m):
+        return pass_copy(g_gu, x_gu, all_gu, xg_s, xg_r, q, m, (feats_of(m), slice(None)))
 
     def down_local(q):
         return pltpu.make_async_copy(g_dn.at[q], all_dn.at[2 * b + q // 2], loc_d.at[q // 2])
@@ -350,31 +368,26 @@
         return pltpu.make_async_copy(g_gu.at[q], all_gu.at[2 * b + q // 2], loc_g.at[q // 2])
 
     def grad_down(q):
-        if q % 2:
-            down_copy(q - 1).wait_recv()
-
         @pl.loop(0, 2)
         def _(m):
-            feats = pl.ds(pl.multiple_of(m * 640, 640), 640)
+            feats = feats_of(m)
             acc = None
             for t in range(4):
                 part = dot_nt(hid[t, q * HC:(q + 1) * HC], xs[1, t // 2, t % 2, feats])
                 acc = part if acc is None else acc + part
             if q % 2:
+                down_copy(q - 1, m).wait_recv()
                 acc = acc + x_dn[q // 2, :, feats].astype(F32)
             g_dn[q, :, feats] = acc.astype(BF16)
-
-        down_copy(q).start()
+            down_copy(q, m).start()
+
         if q % 2:
             down_local(q).start()
 
     def grad_gate_up(q):
-        if q % 2:
-            gu_copy(q - 1).wait_recv()
-
         @pl.loop(0, 2)
         def _(m):
-            feats = pl.ds(pl.multiple_of(m * 640, 640), 640)
+            feats = feats_of(m)
             acc = None
             for t in range(4):
                 both = jnp.concatenate(
@@ -383,10 +396,11 @@
                 part = dot_nt(xs[0, t // 2, t % 2, feats], both)
                 acc = part if acc is None else acc + part
             if q % 2:
+                gu_copy(q - 1, m).wait_recv()
                 acc = acc + x_gu[q // 2, feats, :].astype(F32)
             g_gu[q, feats, :] = acc.astype(BF16)
-
-        gu_copy(q).start()
+            gu_copy(q, m).start()
+
         if q % 2:
             gu_local(q).start()
 
@@ -422,8 +436,24 @@
             if d:
                 sum_y(s, d).start()
 
-    def sum_final(s, i):
-        return remote(o_fin.at[s, i], o_got.at[s, xh], fn_s.at[s, i], fn_r.at[s, xh], spread_from(i))
+    def sum_mid(s, i):
+        to = (b, 2 * i + low, c)
+        return remote(o_fin.at[s, i], o_mid.at[s, zh], md_s.at[s, i], md_r.at[s, zh], to)
+
+    def sum_final(s, h):
+        return remote(o_mid.at[s, h], o_got.at[s, xh], fn_s.at[s, h], fn_r.at[s, xh], in_plane(h))
+
+    def sum_turn(s):
+        for h in range(2):
+            pltpu.make_async_copy(o_fin.at[s, h], o_mid.at[s, h], md_r.at[s, h]).wait()
+
+            @pl.when(jnp.logical_not(same_place(h)))
+            def _(h=h):
+                sum_final(s, h).start()
+
+            @pl.when(same_place(h))
+            def _(h=h):
+                pltpu.make_async_copy(o_mid.at[s, h], o_got.at[s, xh], fn_r.at[s, xh]).start()
 
     def sum_chips(s):
         for d in (1, 3, 2):
@@ -434,79 +464,81 @@
                 total = total + o_y[s, d, i].astype(F32)
             o_fin[s, i] = total.astype(BF16)
 
-            @pl.when(jnp.logical_not(from_self(i)))
+            @pl.when(jnp.logical_not(same_row(i)))
             def _(i=i):
-                sum_final(s, i).start()
-
-            @pl.when(from_self(i))
+                sum_mid(s, i).start()
+
+            @pl.when(same_row(i))
             def _(i=i):
-                pltpu.make_async_copy(o_fin.at[s, i], o_got.at[s, xh], fn_r.at[s, xh]).start()
+                pltpu.make_async_copy(o_fin.at[s, i], o_mid.at[s, zh], md_r.at[s, zh]).start()
 
     def sum_end(s):
         for h in range(2):
-            pltpu.make_async_copy(o_fin.at[s, h], o_got.at[s, h], fn_r.at[s, h]).wait()
+            pltpu.make_async_copy(o_mid.at[s, h], o_got.at[s, h], fn_r.at[s, h]).wait()
 
     gate_up(0)
     gate_up(1)
     gather_pass(1)
     relay(gu_flow, 0)
-    turn_other(1)
-    gate_up(2)
+    gate_up(3)
     relay(gu_flow, 1)
     hidden_step(0)
     gather_last(1)
-    gate_up(3)
-    relay(gu_flow, 2)
+    turn_other(1)
+    gate_up(2)
+    relay(gu_flow, 3)
     hidden_step(1)
     blocks_pass(hid_flow, 0)
     sib_wait_recv(1)
-    weight_copy(0, 2).wait_recv()
-    d_hidden(0)
-    relay(gu_flow, 3)
-    hidden_step(2)
+    d_hidden(1)
+    relay(gu_flow, 2)
+    hidden_step(3)
     blocks_pass(hid_flow, 1)
     blocks_wait(hid_flow, 0)
     grad_down(0)
+    weight_copy(0, 2).wait_recv()
+    d_hidden(0)
+    relay(dh_flow, 1)
+    hidden_step(2)
+    blocks_pass(hid_flow, 3)
+    blocks_wait(hid_flow, 1)
+    blocks_pass(hid_flow, 2)
     weight_copy(1, 2).wait_recv()
-    hidden_step(3)
-    blocks_pass(hid_flow, 2)
-    d_hidden(1)
+    d_hidden(2)
     relay(dh_flow, 0)
+    d_step(1)
     blocks_wait(hid_flow, 2)
     grad_down(2)
-    blocks_pass(hid_flow, 3)
-    d_hidden(2)
-    relay(dh_flow, 1)
-    d_step(0)
-    blocks_wait(hid_flow, 1)
-    grad_down(1)
     blocks_wait(hid_flow, 3)
     turn_down()
     sum_start(0, lambda rows, t: dot_nn(wdt[rows, :], hid[t]))
     d_hidden(3)
     relay(dh_flow, 2)
-    d_step(1)
-    blocks_pass(dgu_flow, 0)
-    grad_down(3)
+    d_step(0)
+    blocks_pass(dgu_flow, 1)
+    grad_down(1)
     sum_cores(0)
     relay(dh_flow, 3)
     d_step(2)
-    blocks_pass(dgu_flow, 1)
+    blocks_pass(dgu_flow, 0)
+    blocks_wait(dgu_flow, 1)
+    d_step(3)
+    blocks_pass(dgu_flow, 2)
     blocks_wait(dgu_flow, 0)
     grad_gate_up(0)
-    d_step(3)
-    blocks_pass(dgu_flow, 2)
-    sum_chips(0)
+    blocks_pass(dgu_flow, 3)
     blocks_wait(dgu_flow, 2)
     grad_gate_up(2)
-    blocks_pass(dgu_flow, 3)
-    blocks_wait(dgu_flow, 1)
+    grad_down(3)
     blocks_wait(dgu_flow, 3)
     sum_start(1, lambda rows, t: dot_nn(wg[rows, :], dgu[t, 0]) + dot_nn(wu[rows, :], dgu[t, 1]))
+    sum_cores(1)
+    sum_chips(0)
     grad_gate_up(1)
-    sum_cores(1)
+    sum_turn(0)
+    sum_chips(1)
     grad_gate_up(3)
-    sum_chips(1)
+    sum_turn(1)
     sum_end(0)
     sum_end(1)
 
@@ -527,20 +559,27 @@
         for i in range(2):
             sum_sib(s, i).wait_send()
 
-            @pl.when(jnp.logical_not(from_self(i)))
+            @pl.when(jnp.logical_not(same_row(i)))
+            def _(s=s, i=i):
+                sum_mid(s, i).wait_send()
+
+            @pl.when(jnp.logical_not(same_place(i)))
             def _(s=s, i=i):
                 sum_final(s, i).wait_send()
 
     for q in range(NQ):
-        down_copy(q).wait_send()
-        gu_copy(q).wait_send()
+        for m in range(2):
+            down_copy(q, m).wait_send()
+            gu_copy(q, m).wait_send()
         if q % 2:
             down_local(q).wait()
             gu_local(q).wait()
-            down_landed = all_dn.at[2 * (1 - b) + q // 2]
-            gu_landed = all_gu.at[2 * (1 - b) + q // 2]
-            remote(g_dn.at[q], down_landed, xd_s.at[q], xd_r.at[q], partner).wait_recv()
-            remote(g_gu.at[q], gu_landed, xg_s.at[q], xg_r.at[q], partner).wait_recv()
+            slot = 2 * (1 - b) + q // 2
+            for m in range(2):
+                down_landed = all_dn.at[slot, :, feats_of(m)]
+                gu_landed = all_gu.at[slot, feats_of(m), :]
+                remote(down_landed, down_landed, xd_s.at[q, m], xd_r.at[q, m], partner).wait_recv()
+                remote(gu_landed, gu_landed, xg_s.at[q, m], xg_r.at[q, m], partner).wait_recv()
     for i in range(2):
         for n in range(3):
             weight_copy(i, n).wait_send()
@@ -584,13 +623,14 @@
             buf(4, HID, TOK), buf(4, 2, HID, TOK), buf(NQ, PANEL, 2 * HC), buf(NQ, HC, PANEL),
             buf(2, PANEL, 2 * HC), buf(2, HC, PANEL),
             buf(2, 2, 2, PANEL, TOK), buf(2, 2, 2, 2, FEAT, TOK), buf(2, 4, 2, FEAT, TOK),
-            buf(2, 3, 2, FEAT, TOK), buf(2, 2, FEAT, TOK),
+            buf(2, 3, 2, FEAT, TOK), buf(2, 2, FEAT, TOK), buf(2, 2, FEAT, TOK),
             dma((2, 3)), dma((2, 3)), dma((2, 3)),
             dma((2, 2)), dma((2, 2)), dma((2, 4)), dma((2, 4)), dma((2, 4)), dma((2, 4)),
             dma((NQ, 6)), dma((NQ, 6)), dma((NQ, 4)), dma((NQ, 4)),
             dma((NQ, 6)), dma((NQ, 6)), dma((NQ, 4)), dma((NQ, 4)),
-            dma((NQ,)), dma((NQ,)), dma((NQ,)), dma((NQ,)), dma((2,)), dma((2,)),
-            dma((2, 2)), dma((2, 2)), dma((2, 3)), dma((2, 3)), dma((2, 2)), dma((2, 2)),
+            dma((NQ, 2)), dma((NQ, 2)), dma((NQ, 2)), dma((NQ, 2)), dma((2,)), dma((2,)),
+            dma((2, 2)), dma((2, 2)), dma((2, 3)), dma((2, 3)),
+            dma((2, 2)), dma((2, 2)), dma((2, 2)), dma((2, 2)),
         ],
         name="layer",
         compiler_params=pltpu.CompilerParams(

time: 162 us -> 156 us (0.963)
  the two profiles are of different devices: /device:TPU:66 before, /device:TPU:34 now
where the time goes in v3:
time: 156 us
  Pallas kernels  155 us (99%)
    pallas_call x1, Pallas kernels, body(): pl.pallas_call(layer_kernel, out_shape=[shape((2, 2, FEAT, TOK), BF16), s...  149 us
    pallas_call x1, Pallas kernels, body(): pl.pallas_call(widen_kernel, grid=(NQ,), out_shape=[shape((PANEL, HID), F...  6.07 us

profile of v3, /device:TPU:34, one launch (start us, length us, event | category | flops | bytes accessed | tf_op | source)
XLA Modules:
  0.0 155.5 jit_solution(16991361485068733766)
XLA Ops:
  0.6 148.8 %layer.1 = (bf16[2,2,320,256]{3,2,1,0:T(8,128)(2,1)}, bf16[4,1280,256]{2,1,0:T(8,128)(2,1)}, bf16[4,128,1280]{2,1,0:T(8,128)(2,1)}) custom-call(bf16[320,256]{1,0:T(8,128)(2,1)} %bitcast.12, bf16[320,256]{1,0:T(8,128)(2,1)} %bitcast.13, bf16[1280,512]{1,0:T(8,128)(2,1)} %wg_in.1, bf16[1280,512]{1,0:T(8,128)(2,1)} %wu_in.1, bf16[512,1280]{1,0:T(8,128)(2,1)} %wd_in.1), custom_call_target="tpu_custom_call" | custom-call | tf_op jit(solution)/shard_map/layer/pallas_call | solution.py:607
  149.5 6.1 %widen.1 = (f32[1280,512]{1,0:T(8,128)}, f32[1280,512]{1,0:T(8,128)}, f32[512,1280]{1,0:T(8,128)}, bf16[320,256]{1,0:T(8,128)(2,1)}, bf16[320,256]{1,0:T(8,128)(2,1)}) custom-call(bf16[4,1280,256]{2,1,0:T(8,128)(2,1)} %get-tuple-element.13.all_gu, bf16[4,128,1280]{2,1,0:T(8,128)(2,1)} %get-tuple-element.14.all_dn, bf16[2,2,320,256]{3,2,1,0:T(8,128)(2,1)} %get-tuple-element.15.got), custom_call_target="tpu_custom_call" | custom-call | tf_op jit(solution)/shard_map/widen/pallas_call | solution.py:645

commit v4 on v3

--- a/solution.py
+++ b/solution.py
@@ -38,7 +38,7 @@
     xs, wg, wu, wd, wgut, wdt,
     p_gu, t_gu, r_gu, o_gu, p_dh, t_dh, r_dh, o_dh, c_gate, c_up,
     hid, dgu, g_gu, g_dn, x_gu, x_dn,
-    o_part, o_sib, o_sum, o_y, o_fin, o_mid,
+    o_part, o_sib, o_sum, o_far, o_y, o_fin, o_mid,
     w_r, wf_s, wf_r,
     p0_s, p0_r, p1_s, p1_r, p2_s, p2_r,
     gu_s, gu_r, hb_s, hb_r, dh_s, dh_r, dg_s, dg_r,
@@ -422,8 +422,18 @@
         for h in range(2):
             sum_terms(s, h, core, product)
 
-    def sum_y(s, d):
-        return remote(o_sum.at[s, d], o_y.at[s, d - 1], yr_s.at[s, d - 1], yr_r.at[s, d - 1], at_y(d))
+    def sum_y(s, slot):
+        i = (0, 1, 1, 0, 0, 1)[slot]
+        src = o_sum.at[s, (2, 2, 1, 3, 1, 3)[slot], i]
+        dst = o_far.at[s, slot] if slot < 2 else o_y.at[s, slot % 2, i]
+        return remote(src, dst, yr_s.at[s, slot], yr_r.at[s, slot], at_y(3 if slot % 2 else 1))
+
+    def sum_relay(s):
+        for slot in (0, 1):
+            sum_y(s, slot).wait_recv()
+            d = 1 + 2 * slot
+            o_sum[s, d, slot] = (o_sum[s, d, slot].astype(F32) + o_far[s, slot].astype(F32)).astype(BF16)
+            sum_y(s, slot + 4).start()
 
     def sum_cores(s):
         for h in range(2):
@@ -433,8 +443,8 @@
             for i in range(2):
                 mine = o_part[s, i, flip(yy // 2, zl), rows_of(2 * (yy % 2) + core), :].astype(F32)
                 o_sum[s, d, i] = (mine + o_sib[s, yy % 2, i, flip(yy // 2, zl)].astype(F32)).astype(BF16)
-            if d:
-                sum_y(s, d).start()
+            for slot in ((), (2,), (0, 1), (3,))[d]:
+                sum_y(s, slot).start()
 
     def sum_mid(s, i):
         to = (b, 2 * i + low, c)
@@ -456,11 +466,11 @@
                 pltpu.make_async_copy(o_mid.at[s, h], o_got.at[s, xh], fn_r.at[s, xh]).start()
 
     def sum_chips(s):
-        for d in (1, 3, 2):
-            sum_y(s, d).wait_recv()
+        for slot in (2, 3, 4, 5):
+            sum_y(s, slot).wait_recv()
         for i in range(2):
             total = o_sum[s, 0, i].astype(F32)
-            for d in range(3):
+            for d in range(2):
                 total = total + o_y[s, d, i].astype(F32)
             o_fin[s, i] = total.astype(BF16)
 
@@ -522,6 +532,7 @@
     d_step(2)
     blocks_pass(dgu_flow, 0)
     blocks_wait(dgu_flow, 1)
+    sum_relay(0)
     d_step(3)
     blocks_pass(dgu_flow, 2)
     blocks_wait(dgu_flow, 0)
@@ -532,9 +543,10 @@
     grad_down(3)
     blocks_wait(dgu_flow, 3)
     sum_start(1, lambda rows, t: dot_nn(wg[rows, :], dgu[t, 0]) + dot_nn(wu[rows, :], dgu[t, 1]))
+    grad_gate_up(1)
     sum_cores(1)
     sum_chips(0)
-    grad_gate_up(1)
+    sum_relay(1)
     sum_turn(0)
     sum_chips(1)
     grad_gate_up(3)
@@ -554,8 +566,8 @@
         for d in range(4):
             sib_copy(s, d).wait_send()
             y_copy(s, d).wait_send()
-        for d in range(1, 4):
-            sum_y(s, d).wait_send()
+        for slot in range(6):
+            sum_y(s, slot).wait_send()
         for i in range(2):
             sum_sib(s, i).wait_send()
 
@@ -623,13 +635,14 @@
             buf(4, HID, TOK), buf(4, 2, HID, TOK), buf(NQ, PANEL, 2 * HC), buf(NQ, HC, PANEL),
             buf(2, PANEL, 2 * HC), buf(2, HC, PANEL),
             buf(2, 2, 2, PANEL, TOK), buf(2, 2, 2, 2, FEAT, TOK), buf(2, 4, 2, FEAT, TOK),
-            buf(2, 3, 2, FEAT, TOK), buf(2, 2, FEAT, TOK), buf(2, 2, FEAT, TOK),
+            buf(2, 2, FEAT, TOK), buf(2, 2, 2, FEAT, TOK),
+            buf(2, 2, FEAT, TOK), buf(2, 2, FEAT, TOK),
             dma((2, 3)), dma((2, 3)), dma((2, 3)),
             dma((2, 2)), dma((2, 2)), dma((2, 4)), dma((2, 4)), dma((2, 4)), dma((2, 4)),
             dma((NQ, 6)), dma((NQ, 6)), dma((NQ, 4)), dma((NQ, 4)),
             dma((NQ, 6)), dma((NQ, 6)), dma((NQ, 4)), dma((NQ, 4)),
             dma((NQ, 2)), dma((NQ, 2)), dma((NQ, 2)), dma((NQ, 2)), dma((2,)), dma((2,)),
-            dma((2, 2)), dma((2, 2)), dma((2, 3)), dma((2, 3)),
+            dma((2, 2)), dma((2, 2)), dma((2, 6)), dma((2, 6)),
             dma((2, 2)), dma((2, 2)), dma((2, 2)), dma((2, 2)),
         ],
         name="layer",

time: 156 us -> 153 us (0.981)
  the two profiles are of different devices: /device:TPU:34 before, /device:TPU:66 now
where the time goes in v4:
time: 153 us; the launch traced here: 151 us
  Pallas kernels  150 us (98%)
    pallas_call x1, Pallas kernels, body(): pl.pallas_call(layer_kernel, out_shape=[shape((2, 2, FEAT, TOK), BF16), s...  144 us
    pallas_call x1, Pallas kernels, body(): pl.pallas_call(widen_kernel, grid=(NQ,), out_shape=[shape((PANEL, HID), F...  6.07 us

profile of v4, /device:TPU:66, one launch (start us, length us, event | category | flops | bytes accessed | tf_op | source)
XLA Modules:
  0.0 150.7 jit_solution(9715438997552123156)
XLA Ops:
  0.6 143.8 %layer.1 = (bf16[2,2,320,256]{3,2,1,0:T(8,128)(2,1)}, bf16[4,1280,256]{2,1,0:T(8,128)(2,1)}, bf16[4,128,1280]{2,1,0:T(8,128)(2,1)}) custom-call(bf16[320,256]{1,0:T(8,128)(2,1)} %bitcast.12, bf16[320,256]{1,0:T(8,128)(2,1)} %bitcast.13, bf16[1280,512]{1,0:T(8,128)(2,1)} %wg_in.1, bf16[1280,512]{1,0:T(8,128)(2,1)} %wu_in.1, bf16[512,1280]{1,0:T(8,128)(2,1)} %wd_in.1), custom_call_target="tpu_custom_call" | custom-call | tf_op jit(solution)/shard_map/layer/pallas_call | solution.py:619
  144.4 6.1 %widen.1 = (f32[1280,512]{1,0:T(8,128)}, f32[1280,512]{1,0:T(8,128)}, f32[512,1280]{1,0:T(8,128)}, bf16[320,256]{1,0:T(8,128)(2,1)}, bf16[320,256]{1,0:T(8,128)(2,1)}) custom-call(bf16[4,1280,256]{2,1,0:T(8,128)(2,1)} %get-tuple-element.13.all_gu, bf16[4,128,1280]{2,1,0:T(8,128)(2,1)} %get-tuple-element.14.all_dn, bf16[2,2,320,256]{3,2,1,0:T(8,128)(2,1)} %get-tuple-element.15.got), custom_call_target="tpu_custom_call" | custom-call | tf_op jit(solution)/shard_map/widen/pallas_call | solution.py:658
